TPU v7x, 32 devices: a whole 2x2x4 slice. The times are simulated.
32 devices in a mesh: dp: 8 (over z, x), fsdp: 4 (over y, core).
Axes of the slice: x: 2, y: 2, z: 4, core: 2. Of those that a mesh axis runs over, the one named last changes fastest.
Arguments:
- tokens: bfloat16 [64, 320, 1024], P(('dp', 'fsdp')), may hold values from -6 to 6
- condition: float32 [3, 1024], replicated, may hold values from -6 to 6
- clip_frames: int32 [3], replicated, may hold values from 2 to 9, as said below
- ada_weight: bfloat16 [1024, 6144], P('fsdp', 'dp'), may hold values from -0.1875 to 0.1875
- ada_bias: bfloat16 [6144], P('dp'), may hold values from -1.796875 to 1.796875
- qkv_weight: bfloat16 [1024, 3072], P('fsdp', 'dp'), may hold values from -0.1875 to 0.1875
- out_weight: bfloat16 [1024, 1024], P('fsdp', 'dp'), may hold values from -0.75 to 0.75
- up_weight: bfloat16 [1024, 4096], P('fsdp', 'dp'), may hold values from -0.1875 to 0.1875
- down_weight: bfloat16 [4096, 1024], P('fsdp', 'dp'), may hold values from -0.09375 to 0.09375
- rel_table: bfloat16 [16, 2025], P('dp'), may hold values from -3 to 3
- cotangent: bfloat16 [64, 320, 1024], P(('dp', 'fsdp')), may hold values from -6 to 6
Outputs:
- output: bfloat16 [64, 320, 1024], P(('dp', 'fsdp'))
- grad_tokens: float32 [64, 320, 1024], P(('dp', 'fsdp'))
- grad_condition: float32 [3, 1024], replicated
- grad_ada_weight: float32 [1024, 6144], P('fsdp', 'dp')
- grad_ada_bias: float32 [6144], P('dp')
- grad_qkv: float32 [1024, 3072], P('fsdp', 'dp')
- grad_out: float32 [1024, 1024], P('fsdp', 'dp')
- grad_up: float32 [1024, 4096], P('fsdp', 'dp')
- grad_down: float32 [4096, 1024], P('fsdp', 'dp')
- grad_table: float32 [16, 2025], P('dp')
Inputs may be any that keep to these rules, and one draw needn't show every extreme that they name: `clip_frames`: A third of the 3 clips, at places drawn from the seed, have 5 + 1 to 9 frames and span two slabs; the others have 2 to 5 frames. Some clip has 2 frames and some 2*5 - 1.
All inputs are finite; a program needn't handle non-finite values.
Results may differ from a plain program's by a relative error of at most 0.018.
The roundings to bfloat16 on the way count: a program that leaves them out, or rounds other values in their place, can miss the bound.
Values may be sent and summed in bfloat16 or wider, within the bound.
A program may use at most 320 MiB of HBM per device.

v0:
```python
import functools

import jax
import jax.numpy as jnp
from jax import lax
from jax.experimental import pallas as pl
from jax.experimental.pallas import tpu as pltpu
from jax.sharding import PartitionSpec as P

D = 1024
H = 16
HD = 64
WT = 5
WSIDE = 8
WIN = 320
SPW = 16
CELLS = WSIDE * WSIDE
FRAMES = 2 * WT - 1
OFFSETS = (2 * WSIDE - 1) ** 2
REL = FRAMES * OFFSETS
LANES = 128
TILE = 256
SPREAD = 80
WIDE = 96
STRIP = 640

EPSILON = 1e-06
NEGATIVE = -1000000000.0
HIGHEST = lax.Precision.HIGHEST
F32 = jnp.float32
BF16 = jnp.bfloat16
MESH = pl.DeviceIdType.MESH
MIB = 2**20

QKV, OUT, UP, DOWN, UNITS = 0, 3, 4, 8, 12
PICK = (
    (1, 2, 0),
    (1, 2, 0),
    (0, 1, 2),
    (0, 1, 2),
    (0, 1, 2),
    (2, 0, 1),
    (2, 0, 1),
    (1, 0, 2),
)
SHARE = 256
HALF = 128


SPLIT = (4, 2, 2, 2, SHARE, LANES)
CLIP_ROWS = 4
MOD_ROWS = 6 * CLIP_ROWS
OWN_SLOTS = 4
ORDER = (0, 1, 2, 3, 4, 8, 5, 9, 6, 10, 7, 11)
GATHER_ASIDE = (DOWN + 3,)
REDUCE_ASIDE = (DOWN, UP + 2)
ENTER = (((2, 1), (0, 1), (11, 1), (11, 2), (2, 2), (1, 1)), ((2, 3), (0, 2), (6, 1), (1, 2)), ((0, 3),), ((1, 3), (5, 1), (3, 1), (6, 2)), ((2, 4), (0, 4), (4, 1), (5, 2)), ((8, 1), (6, 3)))
ATTEND = {0: ((3, 2), (7, 1), (5, 3)), 1: ((1, 4),), 2: ((4, 2), (10, 1)), 3: ((3, 3), (9, 1)), 4: ((4, 3),), 5: ((5, 4),), 6: ((3, 4), (7, 2), (8, 2)), 7: ((4, 4),)}
MIDDLE = {0: ((8, 3), (7, 3), (6, 4)), 2: ((11, 3),), 3: ((10, 2), (9, 2)), 4: ((7, 4), (8, 4)), 5: ((10, 3),), 6: ((9, 3),), 8: ((10, 4),), 9: ((9, 4),), 11: ((11, 4),)}
EARLY = (DOWN, UP, DOWN + 1, UP + 1, DOWN + 2)
DONE = EARLY[:4]
EARLY_POINTS = {7: ((4, 0), (8, 0)), 8: ((4, 1),), 9: ((8, 1),), 10: ((9, 0), (4, 2)), 11: ((9, 1), (5, 0)), 12: ((4, 3),), 13: ((5, 1),), 14: ((10, 0), (9, 2)), 16: ((5, 2),), 17: ((8, 2), (9, 3), (10, 1)), 18: ((8, 3), (5, 3)), 19: ((8, 4), (4, 4)), 20: ((5, 4),), 21: ((10, 2), (9, 4))}
LATE = (UP + 2, DOWN + 3, UP + 3, OUT, QKV, QKV + 1, QKV + 2)
LATE_POINTS = {0: ((6, 0), (10, -3), (11, 0)), 1: ((6, 1), (11, 1)), 2: ((7, 0),), 3: ((3, 0), (7, 1), (11, 2)), 4: ((0, 0), (3, 1), (10, 3)), 6: ((7, 2), (1, 0), (0, 1)), 7: ((11, 3), (3, 2)), 8: ((6, 2), (10, 4), (11, 4)), 10: ((1, 1),), 11: ((7, 3), (3, 3)), 12: ((0, 2),), 13: ((2, 0),), 14: ((2, 1),), 15: ((1, 2),), 16: ((0, 3),), 18: ((1, 3), (6, 3), (2, 2)), 19: ((6, 4), (2, 3)), 20: ((1, 4),), 21: ((3, 4),), 22: ((7, 4),), 24: ((0, 4), (2, 4))}
def reduce_stages(points):
    moves = [move for at in sorted(points) for move in points[at]]
    started = [(unit, 3 if stage == -3 else stage + 1) for unit, stage in moves if stage < 4]
    return [(unit, stage) for unit, stage in started if stage > 3 or (unit, stage) in moves or stage < 3]


def gather_stages(points):
    return [(ORDER[index], stage) for point in points for index, stage in point]


def forward_pair(step):
    first = (13 - step) // 8
    return first * ((step // 2 + 1) % 3 + 3 * (step % 2)) + (1 - first) * step


def backward_pair(step):
    group, place = step // 3, step % 3
    return (1 + group) % 3 + 3 * place - place // 2


def pair_unit(which, pair):
    first = (13 - pair) // 8
    sixth, seventh = ((0, 2, 0), (1, 1, 2))[0][which], ((0, 2, 0), (1, 1, 2))[1][which]
    return first * ((pair + 2) % 3) + (1 - first) * ((7 - pair) * sixth + (pair - 6) * seventh)


def pair_block(which, pair):
    return (which * (H // 2) + pair) // 3


def picked(block, j):
    return sum(jnp.where(block == index, PICK[index][j], 0) for index in range(8))


def window_layout(clip_frames, first_window, window_count):
    slab_count = 1 + (clip_frames > WT).astype(jnp.int32)
    starts = jnp.cumsum(slab_count, dtype=jnp.int32) - slab_count
    global_window = first_window + jnp.arange(window_count, dtype=jnp.int32)
    slab_of = global_window // SPW
    owners = jnp.sum((starts[None, :] <= slab_of[:, None]).astype(jnp.int32), axis=1) - 1
    clip_ids = jnp.arange(clip_frames.shape[0], dtype=jnp.int32)
    member = (owners[:, None] == clip_ids[None, :]).astype(jnp.int32)
    clip_start = jnp.sum(member * starts[None, :], axis=1)
    own_frames = jnp.sum(member * clip_frames[None, :], axis=1)
    inner_slab = slab_of - clip_start
    return (jnp.minimum(own_frames - WT * inner_slab, WT), member)


def offset_spread():
    side_span = 2 * WSIDE - 1
    shape = (OFFSETS, WSIDE * LANES)
    offset = lax.broadcasted_iota(jnp.int32, shape, 0)
    place = lax.broadcasted_iota(jnp.int32, shape, 1)
    own, row, other = place // LANES, place // WSIDE % (LANES // WSIDE), place % WSIDE
    row_diff, col_diff = side_span - 1 - row, own - other + (WSIDE - 1)
    return ((row < side_span) & (row_diff * side_span + col_diff == offset)).astype(BF16)


def spread_table(table):
    heads = table.shape[0]
    by_frame = table.reshape(heads, FRAMES, OFFSETS)[:, ::-1].reshape(heads * FRAMES, OFFSETS)
    spread = jnp.dot(by_frame, offset_spread(), preferred_element_type=F32).astype(BF16)
    spread = spread.reshape(heads, FRAMES * WSIDE, LANES)
    return jnp.pad(spread, ((0, 0), (0, SPREAD - FRAMES * WSIDE), (0, 0)))


def gather_table(spread):
    heads = spread.shape[0]
    by_frame = spread[:, : FRAMES * WSIDE].reshape(heads * FRAMES, WSIDE * LANES)
    sums = lax.dot_general(
        by_frame,
        offset_spread().astype(F32),
        (((1,), (1,)), ((), ())),
        precision=HIGHEST,
        preferred_element_type=F32,
    )
    return sums.reshape(heads, FRAMES, OFFSETS)[:, ::-1].reshape(heads, FRAMES * OFFSETS)


def units_of(qkv, out, up, down):
    return jnp.concatenate(
        [
            jnp.stack(
                [
                    jnp.stack([qkv[:, 384 * b + LANES * PICK[b][j] :][:, :LANES] for b in range(8)])
                    for j in range(3)
                ]
            ),
            out.reshape(D, 8, 1, LANES).transpose(2, 1, 0, 3),
            up.reshape(D, 8, 4, LANES).transpose(2, 1, 0, 3),
            down.reshape(8, 4, LANES, 8, LANES).transpose(1, 3, 0, 2, 4).reshape(4, 8, D, LANES),
        ]
    )


def weights_of(units):
    def columns(part):
        return part.transpose(2, 1, 0, 3).reshape(D, -1)

    down = units[DOWN:].reshape(4, 8, 8, LANES, LANES).transpose(2, 0, 3, 1, 4)
    qkv = [
        units[PICK[block].index(tile), block] for block in range(8) for tile in range(3)
    ]
    return (
        jnp.concatenate(qkv, axis=1),
        columns(units[OUT:UP]),
        columns(units[UP:DOWN]),
        down.reshape(4 * D, D),
    )


def dot(left, right):
    return jnp.dot(left, right, preferred_element_type=F32)


def dot_rows(left, right):
    return lax.dot_general(left, right, (((1,), (1,)), ((), ())), preferred_element_type=F32)


def dot_tokens(left, right):
    return lax.dot_general(left, right, (((0,), (0,)), ((), ())), preferred_element_type=F32)


def half(index):
    return pl.ds(pl.multiple_of(index * 512, 512), 512)


def four_columns(unit, index):
    blocks = [unit[2 * index + x // 2, x % 2].reshape(D, LANES) for x in range(4)]
    return jnp.concatenate(blocks, axis=1)


def half_rows(unit, index):
    blocks = [unit[block // 2, block % 2, index].reshape(512, LANES) for block in range(8)]
    return jnp.concatenate(blocks, axis=1)


def put_columns(unit, index, values):
    for x in range(4):
        unit[2 * index + x // 2, x % 2] = values[:, x * LANES : (x + 1) * LANES].reshape(2, 2, SHARE, LANES)


def loop(count, body):
    def step(index, carry):
        body(index)
        return carry

    lax.fori_loop(0, count, step, 0)


def vmem():
    return pl.BlockSpec(memory_space=pltpu.VMEM)


def anywhere():
    return pl.BlockSpec(memory_space=pl.ANY)


def smem():
    return pl.BlockSpec(memory_space=pltpu.SMEM)


def shape(dtype, *sizes):
    return jax.ShapeDtypeStruct(sizes, dtype)


def params(collective=None, limit=58):
    if collective is None:
        return pltpu.CompilerParams(vmem_limit_bytes=limit * MIB)
    return pltpu.CompilerParams(
        vmem_limit_bytes=limit * MIB, collective_id=collective, has_side_effects=True
    )


def centered(values):
    center = values - jnp.mean(values, axis=-1, keepdims=True)
    spread = jnp.mean(center * center, axis=-1, keepdims=True)
    root = lax.rsqrt(spread + EPSILON)
    return center * root, root


def norm_back(grad_normed, normal, root, scale):
    grad = grad_normed * (1.0 + scale)
    mean = jnp.mean(grad, axis=-1, keepdims=True)
    along = jnp.mean(grad * normal, axis=-1, keepdims=True)
    return root * (grad - mean - normal * along)


def each_rows(mod_ref, live_ref, body, rows=32, pump=lambda window: None):
    for window in range(mod_ref.shape[0]):
        live = live_ref[window] * CELLS

        def step(index, window=window, live=live):
            at = pl.ds(pl.multiple_of(window * WIN + index * rows, rows), rows)
            mods = [mod_ref[window, k : k + 1, :] for k in range(6)]
            slot = index * rows + lax.broadcasted_iota(jnp.int32, (rows, 1), 0)
            body(window, at, mods, slot < live)

        loop(WIN // rows, step)
        pump(window)


def add_sums(sums_ref, window, which, values):
    sums_ref[window, which : which + 1, :] += jnp.sum(values, axis=0, keepdims=True)


class Place:
    def __init__(self):
        column, row = lax.axis_index("dp"), lax.axis_index("fsdp")
        self.z, self.x, self.y, self.c = column // 2, column % 2, row // 2, row % 2

    def at(self, z=None, x=None, y=None, c=None):
        z = self.z if z is None else z
        x = self.x if x is None else x
        y = self.y if y is None else y
        c = self.c if c is None else c
        return (z * 2 + x, y * 2 + c)

    def far(self, k):
        return lax.rem(self.z + k, 4)

    def shifted(self, dz, dx, dy, dc):
        def other(index, change):
            return 1 - index if change else index

        return self.at(self.far(dz), other(self.x, dx), other(self.y, dy), other(self.c, dc))

    def greet(self, far_ones=()):
        near = [(1, 0, 0, 0), (2, 0, 0, 0), (3, 0, 0, 0), (0, 1, 0, 0), (0, 0, 1, 0), (0, 0, 0, 1)]
        peers = near + [change for change in far_ones if change not in near]
        barrier = pltpu.get_barrier_semaphore()
        for change in peers:
            pl.semaphore_signal(
                barrier, inc=1, device_id=self.shifted(*change), device_id_type=MESH
            )
        pl.semaphore_wait(barrier, len(peers))


EVERYONE = [
    (dz, dx, dy, dc)
    for dz in range(4)
    for dx in range(2)
    for dy in range(2)
    for dc in range(2)
    if (dz, dx, dy, dc) != (0, 0, 0, 0)
]
ALONG_ZX = [change for change in EVERYONE if change[2:] == (0, 0)]
ALONG_YC = [change for change in EVERYONE if change[:2] == (0, 0)]


class Moves:
    def __init__(self, place, stages, scratch):
        self.place = place
        self.send, self.recv = scratch
        self.first, count = {}, 0
        for unit, stage in stages:
            self.first[unit, stage] = count
            count += self.counts[unit in self.aside][stage - 1]
        self.flying = []

    @classmethod
    def semaphores(cls, stages):
        count = sum(cls.counts[unit in cls.aside][stage - 1] for unit, stage in stages)
        return [pltpu.SemaphoreType.DMA((count,))] * 2

    def made(self, unit, stage, moves):
        copies = []
        for index, (source, target, device) in enumerate(moves):
            slot = self.first[unit, stage] + index
            copies.append(
                pltpu.make_async_remote_copy(
                    src_ref=source,
                    dst_ref=target,
                    send_sem=self.send.at[slot],
                    recv_sem=self.recv.at[slot],
                    device_id=device,
                    device_id_type=MESH,
                )
            )
        return copies

    def begin(self, unit, stage):
        for copy in self.copies(unit, stage):
            copy.start()
        self.flying.append((unit, stage))

    def arrive(self, unit, stage):
        if (unit, stage) in self.flying:
            self.flying.remove((unit, stage))
            for copy in self.copies(unit, stage):
                copy.wait_recv()

    def sent(self):
        for unit, stage in self.first:
            for copy in self.copies(unit, stage):
                copy.wait_send()


class Gather(Moves):
    counts = ((3, 2, 2, 1), (2, 2, 3, 1))
    aside = GATHER_ASIDE

    def __init__(self, place, held, stages, scratch):
        super().__init__(place, stages, scratch)
        self.held = held

    def copies(self, unit, stage):
        p, held = self.place, self.held.at[unit]
        at_x, at_y, at_core = p.at(x=1 - p.x), p.at(y=1 - p.y), p.at(c=1 - p.c)
        own = held.at[p.z, p.x, p.y, p.c]
        if stage == 4:
            refs = [(held.at[:, :, :, p.c], at_core)]
        elif unit in self.aside and stage == 1:
            refs = [(own.at[:HALF], at_x), (own.at[HALF:], at_y)]
        elif unit in self.aside and stage == 2:
            refs = [
                (held.at[p.z, :, p.y, p.c, :HALF], at_y),
                (held.at[p.z, p.x, :, p.c, HALF:], at_x),
            ]
        elif unit in self.aside:
            refs = [(held.at[p.z, :, :, p.c], p.at(z=p.far(k))) for k in (1, 2, 3)]
        elif stage == 1:
            refs = [(own, p.at(z=p.far(k))) for k in (1, 2, 3)]
        elif stage == 2:
            refs = [
                (held.at[:, p.x, p.y, p.c, :HALF], at_x),
                (held.at[:, p.x, p.y, p.c, HALF:], at_y),
            ]
        else:
            refs = [
                (held.at[:, :, p.y, p.c, :HALF], at_y),
                (held.at[:, p.x, :, p.c, HALF:], at_x),
            ]
        return self.made(unit, stage, [(ref, ref, device) for ref, device in refs])

    def advance(self, unit, stage):
        self.arrive(unit, stage - 1)
        self.begin(unit, stage)

    def finish(self):
        for unit, stage in list(self.flying):
            self.arrive(unit, stage)
        self.sent()


class Reduce(Moves):
    counts = ((1, 2, 2, 3), (1, 3, 2, 2))
    aside = REDUCE_ASIDE

    def __init__(self, place, part, points, store, buffers, scratch):
        super().__init__(place, reduce_stages(points), scratch[2:])
        self.part, self.store, self.buffers = part, store, buffers
        self.own, self.load = scratch[:2]
        self.slots, self.loaded = {}, []

    @classmethod
    def scratch(cls, points):
        return [
            pltpu.VMEM((OWN_SLOTS, 4, 2, 2, SHARE, LANES), BF16),
            pltpu.SemaphoreType.DMA((OWN_SLOTS,)),
        ] + cls.semaphores(reduce_stages(points))

    @staticmethod
    def core_shape(count):
        return (count, 4, 2, 2, SHARE, LANES)

    @staticmethod
    def side_shape(count):
        return (count, 2, 4, 2, HALF, LANES)

    @staticmethod
    def corner_shape(count):
        return (count, 2, 4, HALF, LANES)

    @staticmethod
    def distant_shape(count):
        return (count, 3, 2, HALF, LANES)

    @staticmethod
    def aside_shape(count):
        return (count, 3, 2, 2, SHARE, LANES)

    def own_copy(self, unit):
        slot = self.slots.setdefault(unit, len(self.slots) % OWN_SLOTS)
        return pltpu.make_async_copy(
            self.part(unit).at[:, :, :, self.place.c], self.own.at[slot], self.load.at[slot]
        )

    def copies(self, unit, stage):
        p = self.place
        at_x, at_y, at_core = p.at(x=1 - p.x), p.at(y=1 - p.y), p.at(c=1 - p.c)
        core, side, corner, distant = self.buffers(unit)
        if unit in self.aside and stage == 2:
            moves = [
                (core.at[p.far(k)], distant.at[k - 1], p.at(z=p.far(k))) for k in (1, 2, 3)
            ]
        elif unit in self.aside and stage == 3:
            moves = [
                (core.at[p.z, :, 1 - p.y, :HALF], side.at[0, 0], at_y),
                (core.at[p.z, 1 - p.x, :, HALF:], side.at[1, 0], at_x),
            ]
        elif unit in self.aside and stage == 4:
            moves = [
                (side.at[0, 0, 1 - p.x], side.at[0, 1, 0], at_x),
                (side.at[1, 0, 1 - p.y], side.at[1, 1, 0], at_y),
            ]
        elif stage == 1:
            moves = [(self.part(unit).at[:, :, :, 1 - p.c], core, at_core)]
        elif stage == 2:
            moves = [
                (core.at[:, :, 1 - p.y, :HALF], side.at[0], at_y),
                (core.at[:, 1 - p.x, :, HALF:], side.at[1], at_x),
            ]
        elif stage == 3:
            moves = [
                (side.at[0, :, 1 - p.x], corner.at[0], at_x),
                (side.at[1, :, 1 - p.y], corner.at[1], at_y),
            ]
        else:
            moves = [
                (corner.at[:, p.far(k)], distant.at[k - 1], p.at(z=p.far(k))) for k in (1, 2, 3)
            ]
        return self.made(unit, stage, moves)

    def begin(self, unit, stage):
        super().begin(unit, stage)
        if stage == 1:
            self.own_copy(unit).start()
            assert self.slots[unit] not in self.loaded
            self.loaded.append(self.slots[unit])

    def combine(self, unit, stage):
        p = self.place
        core, side, corner, distant = self.buffers(unit)

        def plus(left, right):
            return (left.astype(F32) + right.astype(F32)).astype(BF16)

        def from_core(step):
            z, x, y = step // 4, step // 2 % 2, step % 2
            core[z, x, y] = plus(core[z, x, y], self.own[self.slots[unit], z, x, y])

        def from_side(step):
            z, b = step // 2, step % 2
            side[0, z, b] = plus(side[0, z, b], core[z, b, p.y, :HALF])
            side[1, z, b] = plus(side[1, z, b], core[z, p.x, b, HALF:])

        def from_corner(z):
            corner[0, z] = plus(corner[0, z], side[0, z, p.x])
            corner[1, z] = plus(corner[1, z], side[1, z, p.y])

        def from_far(half):
            total = corner[half, p.z].astype(F32)
            for k in range(3):
                total = total + distant[k, half].astype(F32)
            self.store(unit, half, total)

        def aside_far(step):
            x, y = step // 2, step % 2
            total = core[p.z, x, y].astype(F32)
            for k in range(3):
                total = total + distant[k, x, y].astype(F32)
            core[p.z, x, y] = total.astype(BF16)

        def aside_side(b):
            side[0, 0, b] = plus(side[0, 0, b], core[p.z, b, p.y, :HALF])
            side[1, 0, b] = plus(side[1, 0, b], core[p.z, p.x, b, HALF:])

        if unit in self.aside and stage == 4:
            for part, own in enumerate((p.x, p.y)):
                total = side[part, 0, own].astype(F32) + side[part, 1, 0].astype(F32)
                self.store(unit, part, total)
            return
        steps = {1: (16, from_core), 2: (8, from_side), 3: (4, from_corner), 4: (2, from_far)}
        if unit in self.aside:
            steps |= {2: (4, aside_far), 3: (2, aside_side)}
        loop(*steps[stage])

    def step(self, unit, stage):
        if stage <= 0:
            self.begin(unit, max(1, -stage))
            return
        self.arrive(unit, stage)
        if stage == 1:
            self.own_copy(unit).wait()
        self.combine(unit, stage)
        if stage == 1:
            self.loaded.remove(self.slots[unit])
        if (unit, stage + 1) in self.first:
            self.begin(unit, stage + 1)


class Copies:
    def __init__(self, send, recv):
        self.send, self.recv, self.count = send, recv, 0

    def __call__(self, source, target, device):
        slot = self.count
        self.count += 1
        copy = pltpu.make_async_remote_copy(
            src_ref=source,
            dst_ref=target,
            send_sem=self.send.at[slot],
            recv_sem=self.recv.at[slot],
            device_id=device,
            device_id_type=MESH,
        )
        copy.start()
        return copy


class Refs:
    pass


def call(kernel, name, inputs, outputs, scratch, aliases=(), collective=None, grid=None, limit=58):
    names = list(inputs) + list(outputs)
    flat = []
    for value in scratch.values():
        flat += value if isinstance(value, list) else [value]

    def body(*refs):
        held = Refs()
        rest = list(refs)
        for key in names:
            setattr(held, key, rest.pop(0))
        for key, value in scratch.items():
            if isinstance(value, list):
                setattr(held, key, [rest.pop(0) for _ in value])
            else:
                setattr(held, key, rest.pop(0))
        kernel(held)

    extra = {} if grid is None else {"grid": grid}
    made = functools.partial(
        pl.pallas_call,
        body,
        in_specs=[spec for _, spec in inputs.values()],
        out_specs=[spec for _, spec in outputs.values()],
        out_shape=[out for out, _ in outputs.values()],
        scratch_shapes=flat,
        input_output_aliases={
            list(inputs).index(one): list(outputs).index(other) for one, other in aliases
        },
        compiler_params=params(collective, limit),
        name=name,
        **extra,
    )
    arrays = [array for array, _ in inputs.values()]
    if name == "start":
        result = made()(*arrays)
    else:
        result = made()(*arrays)
    out = Refs()
    for key, value in zip(outputs, result, strict=True):
        setattr(out, key, value)
    return out


def enter_norm(refs, pump=lambda: None):
    rows = 32
    for window in range(refs.mod.shape[0]):
        shift, scale = refs.mod[window, 0:1, :], refs.mod[window, 1:2, :]

        def step(index, window=window, shift=shift, scale=scale):
            at = pl.ds(pl.multiple_of(window * WIN + index * rows, rows), rows)
            normal, _ = centered(refs.tokens[at, :].astype(F32))
            refs.normed[at, :] = (normal * (1.0 + scale) + shift).astype(BF16)

        loop(WIN // rows, step)
        pump()


def enter_unit(refs, j, held, put=False):
    unit = refs.units.at[0]
    fetch = pltpu.make_async_copy(held, unit, refs.fetches.at[0])
    fetch.start()
    fetch.wait()

    def project(index):
        refs.packed[j, :, half(index)] = dot(refs.normed[...], four_columns(unit, index)).astype(
            BF16
        )

    loop(2, project)
    if put:
        packed_copy(refs, j).start()


def normed_copy(refs):
    return pltpu.make_async_copy(refs.normed, refs.normed_out, refs.packed_sem.at[3])


def packed_copy(refs, j):
    return pltpu.make_async_copy(refs.packed.at[j], refs.packed_out.at[j], refs.packed_sem.at[j])


def enter_plain_kernel(refs):
    enter_norm(refs)
    for j in range(3):
        enter_unit(refs, j, refs.held.at[QKV + j])


def act_rows(refs, place):
    first = (place.y * 2 + place.c) * SHARE
    value = refs.condition[:, pl.ds(pl.multiple_of(first, SHARE), SHARE)]
    act = value / (1.0 + jnp.exp(-value))
    return jnp.concatenate([act, jnp.zeros((8 - value.shape[0], SHARE), F32)], axis=0).astype(BF16)


def enter_layout(refs):
    windows, clips = refs.member.shape[0], refs.condition.shape[0]
    frames = [refs.frames[clip] for clip in range(clips)]
    starts = [0]
    for count in frames:
        starts.append(starts[-1] + 1 + jnp.where(count > WT, 1, 0))
    device = lax.axis_index("dp") * lax.axis_size("fsdp") + lax.axis_index("fsdp")
    refs.member[...] = jnp.zeros_like(refs.member)
    for window in range(windows):
        slab = (device * windows + window) // SPW
        live = 0
        for clip in range(clips):
            mine = starts[clip] <= slab
            if clip < clips - 1:
                mine = mine & (slab < starts[clip + 1])
            inner = frames[clip] - WT * (slab - starts[clip])
            live = live + jnp.where(mine, jnp.minimum(inner, WT), 0)
            refs.member[window, clip : clip + 1, :] = jnp.full(
                (1, LANES), jnp.where(mine, 1.0, 0.0), F32
            )
        refs.live[window] = live


def enter_table(refs):
    refs.rows[...] = jnp.zeros_like(refs.rows)
    table = refs.rel_table[...].astype(F32)
    for head in range(2):
        for frame in range(FRAMES):
            first = (FRAMES - 1 - frame) * OFFSETS
            row = head * (SPREAD // WSIDE) + frame
            refs.rows[row : row + 1, :OFFSETS] = table[head : head + 1, first : first + OFFSETS]
    shape_of = (TILE, WSIDE * LANES)
    offset = lax.broadcasted_iota(jnp.int32, shape_of, 0)
    place = lax.broadcasted_iota(jnp.int32, shape_of, 1)
    own, row, other = place // LANES, place // WSIDE % (LANES // WSIDE), place % WSIDE
    side_span = 2 * WSIDE - 1
    row_diff, col_diff = side_span - 1 - row, own - other + (WSIDE - 1)
    same = (row < side_span) & (row_diff * side_span + col_diff == offset)
    spread = dot(refs.rows[...].astype(BF16), jnp.where(same, 1.0, 0.0).astype(BF16))
    count = 2 * SPREAD // WSIDE
    for own in range(WSIDE):
        refs.spread[pl.ds(own, count, stride=WSIDE), :] = spread[
            :count, own * LANES : (own + 1) * LANES
        ]
    for head in range(2):
        refs.table_own[head] = refs.spread[head * SPREAD : (head + 1) * SPREAD, :].astype(BF16)


def enter(refs, place, work):
    place.greet(ALONG_ZX + ALONG_YC)
    z, x, y, c = place.z, place.x, place.y, place.c
    small = Copies(*refs.small)
    mods = dot(act_rows(refs, place), refs.ada[...])
    mods = mods + jnp.where((y == 0) & (c == 0), 1.0, 0.0) * refs.bias_in[...].astype(F32)
    for block in range(6):
        refs.mod_part[block * CLIP_ROWS : (block + 1) * CLIP_ROWS, :] = mods[
            :CLIP_ROWS, block * LANES : (block + 1) * LANES
        ]
    refs.mod_parts[y, c] = refs.mod_part[...]
    parts = [
        small(refs.mod_part, refs.mod_parts.at[y, c], place.shifted(*change)) for change in ALONG_YC
    ]
    own = []
    for unit in range(UNITS):
        if unit < OUT:
            first = picked(z * 2 + x, unit) * LANES
            refs.own[unit] = refs.qkv[:, pl.ds(pl.multiple_of(first, LANES), LANES)]
        elif unit >= DOWN:
            first = (unit - DOWN) * LANES
            for half in range(2):
                at = slice(half * 512 + first, half * 512 + first + LANES)
                refs.own[unit, half * HALF : (half + 1) * HALF] = refs.down[at, :]
        else:
            source, start = (refs.out, OUT) if unit < UP else (refs.up, UP)
            first = (unit - start) * LANES
            refs.own[unit] = source[:, first : first + LANES]
        own.append(
            pltpu.make_async_copy(
                refs.own.at[unit], refs.held.at[unit, z, x, y, c], refs.own_sem.at[unit]
            )
        )
        own[-1].start()
    points = list(ENTER)

    loaded = []

    def load(unit):
        if unit not in loaded:
            own[unit].wait()
            loaded.append(unit)

    def tick():
        for index, stage in points.pop(0):
            if stage == 1:
                load(ORDER[index])
            work.advance(ORDER[index], stage)

    tick()
    enter_layout(refs)
    enter_table(refs)
    refs.table[z, x, c] = refs.table_own[c]
    for copy in parts:
        copy.wait()
    refs.mods[z, x] = (
        refs.mod_parts[0, 0] + refs.mod_parts[0, 1] + refs.mod_parts[1, 0] + refs.mod_parts[1, 1]
    )
    mods = [
        small(refs.mods.at[z, x], refs.mods.at[z, x], place.shifted(*change))
        for change in ALONG_ZX
    ]
    for unit in range(UNITS):
        load(unit)
    tick()
    for copy in mods:
        copy.wait()
    tables = [
        small(refs.table.at[z, x, c], refs.table.at[z, x, c], place.shifted(*change))
        for change in ALONG_ZX
    ]
    for window in range(refs.mod.shape[0]):
        for block in range(48):
            which, column = divmod(block, 8)
            first = block % 6 * CLIP_ROWS
            part = refs.mods[block // 12, block // 6 % 2, first : first + CLIP_ROWS, :]
            refs.mod[window, which : which + 1, column * LANES : (column + 1) * LANES] = jnp.sum(
                part * refs.member[window], axis=0, keepdims=True
            )
    tick()
    enter_norm(refs, tick)
    normed_copy(refs).start()
    for copy in tables:
        copy.wait()
    last = small(refs.table.at[:, :, c], refs.table.at[:, :, c], place.at(c=1 - c))
    work.arrive(QKV, 4)
    tick()
    enter_unit(refs, 0, refs.held.at[QKV], put=True)
    last.wait()


def attend_pair(refs, table, part, put):
    for head in range(2):
        spread = table(head).astype(F32)
        for frame in range(FRAMES):
            block = spread[frame * WSIDE : (frame + 1) * WSIDE]
            for row in range(WSIDE):
                first = (WSIDE - 1 - row) * WSIDE
                refs.strip[
                    head, row * WSIDE : (row + 1) * WSIDE, frame * CELLS : (frame + 1) * CELLS
                ] = block[:, first : first + CELLS]
        for frame in range(WT):
            first = (WT - 1 - frame) * CELLS
            refs.bias[head, frame * CELLS : (frame + 1) * CELLS, :] = refs.strip[
                head, :, first : first + WIN
            ]
    for window in range(refs.live.shape[0]):
        rows = slice(window * WIN, (window + 1) * WIN)
        live = refs.live[window] * CELLS
        key_live = lax.broadcasted_iota(jnp.int32, (1, WIN), 1) < live
        query, key, value = (part(which, rows) for which in range(3))
        mixed = []
        for head in range(2):
            lanes = slice(head * HD, (head + 1) * HD)
            scores = dot_rows(query[:, lanes] * BF16(HD ** (-0.5)), key[:, lanes]) + refs.bias[head]
            scores = jnp.where(key_live, scores, NEGATIVE)
            shifted = jnp.exp(scores - jnp.max(scores, axis=-1, keepdims=True))
            totals = jnp.sum(shifted, axis=-1, keepdims=True)
            probs = (shifted * (1.0 / totals)).astype(BF16)
            refs.probs[window, head] = probs
            mixed.append(dot(probs, value[:, lanes]).astype(BF16))
        put(rows, jnp.concatenate(mixed, axis=1))


def attend_plain_kernel(refs):
    sources = (refs.query, refs.key, refs.value)

    def put(rows, values):
        refs.mixed[rows, :] = values

    attend_pair(
        refs, lambda head: refs.table[head], lambda which, rows: sources[which][rows, :], put
    )


def start_kernel(refs):
    step = pl.program_id(0)
    pairs = H // 2
    place = Place()
    work = Gather(place, refs.held, gather_stages(ENTER + tuple(ATTEND.values())), refs.gather)

    @pl.when(step == 0)
    def _():
        enter(refs, place, work)

    for at in range(pairs):

        @pl.when(step == at + 1)
        def _(at=at):
            for index, stage in ATTEND.get(at, ()):
                work.advance(ORDER[index], stage)
            if at in (2, 4):
                work.arrive(QKV + at // 2, 4)
                enter_unit(refs, at // 2, refs.held.at[QKV + at // 2], put=True)

    @pl.when((step > 0) & (step <= pairs))
    def _():
        pair = forward_pair(jnp.clip(step - 1, 0, pairs - 1))

        def columns(block):
            return pl.ds(pl.multiple_of(block * LANES, LANES), LANES)

        def part(which, rows):
            return refs.packed[pair_unit(which, pair), rows, columns(pair_block(which, pair))]

        def table(head):
            return refs.table[pair // 2, pair % 2, head]

        def put(rows, values):
            refs.mixed[rows, columns(pair)] = values

        attend_pair(refs, table, part, put)

    @pl.when(step == pairs)
    def _():
        for j in range(3):
            packed_copy(refs, j).wait()
        normed_copy(refs).wait()
        mixed = pltpu.make_async_copy(refs.mixed, refs.mixed_out, refs.packed_sem.at[4])
        mixed.start()
        mixed.wait()
        work.finish()


def packed_block(which, rows, pair):
    return pl.BlockSpec(
        (None, rows, LANES),
        lambda step: (pair_unit(which, pair(step)), 0, pair_block(which, pair(step))),
    )


def attend_back_pair(refs, pair):
    scale = BF16(HD ** (-0.5))
    refs.spread[...] = jnp.zeros_like(refs.spread)
    refs.strip[...] = jnp.zeros_like(refs.strip)
    windows = refs.probs.shape[0]
    results = [[[None] * windows for _ in range(2)] for _ in range(3)]
    for head in range(2):
        lanes = slice(head * HD, (head + 1) * HD)
        bias = None
        for window in range(windows):
            rows = slice(window * WIN, (window + 1) * WIN)
            grad = refs.grad[rows, lanes]
            probs = refs.probs[window, head]
            results[2][head][window] = dot_tokens(grad, probs).T.astype(BF16)
            grad_probs = dot_rows(grad, refs.value[rows, lanes])
            weight = probs.astype(F32)
            product = weight * grad_probs
            total = jnp.sum(product, axis=-1, keepdims=True)
            grad_scores = (product - weight * total).astype(BF16)
            wide = grad_scores.astype(F32)
            bias = wide if bias is None else bias + wide
            results[0][head][window] = dot(grad_scores, refs.key[rows, lanes] * scale).astype(BF16)
            query = refs.query[rows, lanes] * scale
            results[1][head][window] = dot_tokens(query, grad_scores).T.astype(BF16)
        for frame in range(WT):
            first = (WT - 1 - frame) * CELLS
            refs.strip[head, :, first : first + WIN] += bias[frame * CELLS : (frame + 1) * CELLS]
        for frame in range(FRAMES):
            for row in range(WSIDE):
                first = (WSIDE - 1 - row) * WSIDE
                refs.spread[
                    head, frame * WSIDE : (frame + 1) * WSIDE, first : first + CELLS
                ] += refs.strip[
                    head, row * WSIDE : (row + 1) * WSIDE, frame * CELLS : (frame + 1) * CELLS
                ]
    for part in range(3):
        lanes = pl.ds(pl.multiple_of(pair_block(part, pair) * LANES, LANES), LANES)
        for window in range(windows):
            rows = slice(window * WIN, (window + 1) * WIN)
            both = [results[part][head][window] for head in range(2)]
            refs.grad_packed[pair_unit(part, pair), rows, lanes] = jnp.concatenate(both, axis=1)


def middle(refs, place=None, gathering=None):
    order = [OUT] + [unit for j in range(4) for unit in (UP + j, DOWN + j)] + [OUT]
    activated, grad_hidden, grad_low = (refs.packed.at[index] for index in range(3))
    reducing = None
    points = {}
    waiting = set()
    if gathering is not None:

        def buffers(unit):
            index = EARLY.index(unit)
            core, side = refs.core.at[index], refs.side.at[index]
            if unit not in DONE:
                return core, side, None, None
            if unit in REDUCE_ASIDE:
                return core, side, None, refs.aside.at[0]
            return core, side, refs.corner.at[index], refs.distant.at[index]

        def store(unit, part, values):
            at = pl.ds(pl.multiple_of(part * HALF, HALF), HALF)
            refs.total[DONE.index(unit), at, :] = values

        reducing = Reduce(
            place, lambda unit: refs.part.at[unit], EARLY_POINTS, store, buffers, refs.reduce
        )
        for stages in MIDDLE.values():
            waiting |= {ORDER[index] for index, stage in stages if stage == 4}
        points = {at: list(moves) for at, moves in EARLY_POINTS.items()}

    count = [0]

    def pump():
        for index, stage in MIDDLE.get(count[0], ()) if gathering is not None else ():
            gathering.advance(ORDER[index], stage)
            if stage == 4:
                waiting.discard(ORDER[index])
        for unit, stage in points.pop(count[0], ()):
            reducing.step(unit, stage)
        count[0] += 1

    def fetch(step):
        return pltpu.make_async_copy(
            refs.held.at[order[step]], refs.units.at[step % 4], refs.fetches.at[step % 4]
        )

    def start_fetch(step):
        if gathering is not None:
            assert order[step] not in waiting
            gathering.arrive(order[step], 4)
        fetch(step).start()

    def put(slot, unit):
        return pltpu.make_async_copy(refs.made.at[slot], refs.part.at[unit], refs.made_sem.at[slot])

    for step in range(3):
        start_fetch(step)
    pump()
    refs.sums[...] = jnp.zeros_like(refs.sums)
    refs.mlp[...] = jnp.zeros_like(refs.mlp)
    refs.grad_normed[...] = jnp.zeros_like(refs.grad_normed)
    fetch(0).wait()

    def project(index):
        refs.attended[:, half(index)] = dot(refs.mixed[...], four_columns(refs.units.at[0], index))

    loop(2, project)
    pump()

    def modulate(window, at, mods, live):
        middle = refs.tokens[at, :].astype(F32) + mods[2] * refs.attended[at, :]
        normal, _ = centered(middle)
        refs.normed[at, :] = (normal * (1.0 + mods[4]) + mods[3]).astype(BF16)
        grad = jnp.where(live, refs.cotangent[at, :].astype(F32), 0.0)
        grad_low[at, :] = (mods[5] * grad).astype(BF16)

    each_rows(refs.mod, refs.live, modulate)
    pump()
    for j in range(4):
        step = 1 + 2 * j
        up, down = refs.units.at[step % 4], refs.units.at[(step + 1) % 4]
        fetch(step).wait()
        fetch(step + 1).wait()
        start_fetch(step + 2)

        def hide(index, up=up, down=down):
            hidden = dot(refs.normed[...], four_columns(up, index))
            bend = jnp.tanh(0.7978845608028654 * (hidden + 0.044715 * hidden * hidden * hidden))
            activated[:, half(index)] = (0.5 * hidden * (1.0 + bend)).astype(BF16)
            slope = 0.5 * (1.0 + bend) + 0.5 * hidden * (1.0 - bend * bend) * (
                0.7978845608028654 * (1.0 + 3.0 * 0.044715 * hidden * hidden)
            )
            grad_activated = dot_rows(grad_low[...], half_rows(down, index))
            grad_hidden[:, half(index)] = (grad_activated * slope).astype(BF16)

        loop(2, hide)
        if j > 0:
            put(1, UP + j - 1).wait()
        pump()

        def down_gradient(index):
            made = dot_tokens(activated[:, half(index)], grad_low[...]).astype(BF16)
            for block in range(8):
                refs.made[0, block // 2, block % 2, index] = made[
                    :, block * LANES : (block + 1) * LANES
                ].reshape(2, SHARE, LANES)

        loop(2, down_gradient)
        put(0, DOWN + j).start()
        pump()

        def up_gradient(index):
            made = dot_tokens(refs.normed[...], grad_hidden[:, half(index)]).astype(BF16)
            put_columns(refs.made.at[1], index, made)

        loop(2, up_gradient)
        put(0, DOWN + j).wait()
        put(1, UP + j).start()
        pump()
        if j < 3:
            start_fetch(step + 3)

        def out_of_mlp(index, up=up, down=down):
            refs.mlp[:, half(index)] += dot(activated[...], four_columns(down, index))
            refs.grad_normed[:, half(index)] += dot_rows(
                grad_hidden[...], half_rows(up, index)
            )

        loop(2, out_of_mlp)
        pump()

    put(1, UP + 3).wait()

    def join(window, at, mods, live):
        attended = refs.attended[at, :]
        middle = refs.tokens[at, :].astype(F32) + mods[2] * attended
        normal, root = centered(middle)
        mlp = refs.mlp[at, :]
        refs.normed[at, :] = jnp.where(live, middle + mods[5] * mlp, 0.0).astype(BF16)
        grad_result = jnp.where(live, refs.cotangent[at, :].astype(F32), 0.0)
        grad_normed = refs.grad_normed[at, :]
        grad_middle = grad_result + norm_back(grad_normed, normal, root, mods[4])
        refs.mlp[at, :] = grad_middle
        grad_low[at, :] = (mods[2] * grad_middle).astype(BF16)
        add_sums(refs.sums, window, 2, grad_middle * attended)
        add_sums(refs.sums, window, 3, grad_normed)
        add_sums(refs.sums, window, 4, grad_normed * normal)
        add_sums(refs.sums, window, 5, grad_result * mlp)

    each_rows(refs.mod, refs.live, join)
    results = [
        pltpu.make_async_copy(source, target, refs.result_sem.at[index])
        for index, (source, target) in enumerate(
            (
                (refs.normed, refs.output),
                (refs.mlp, refs.grad_middle),
                (activated, refs.grad_mixed),
            )
        )
    ]
    results[0].start()
    results[1].start()
    pump()
    fetch(9).wait()

    def back(index):
        made = dot_tokens(refs.mixed[...], grad_low[:, half(index)]).astype(BF16)
        put_columns(refs.made.at[0], index, made)
        activated[:, half(index)] = dot_rows(
            grad_low[...], half_rows(refs.units.at[1], index)
        ).astype(BF16)

    loop(2, back)
    results[2].start()
    put(0, OUT).start()
    put(0, OUT).wait()
    while points:
        pump()
    for index, unit in enumerate(EARLY if gathering is not None else ()):
        if unit not in DONE:

            def keep(z, index=index):
                for part in range(2):
                    refs.side_out[index - len(DONE), part, z] = refs.side[index, part, z]

            loop(4, keep)
    for copy in results:
        copy.wait()
    if gathering is not None:
        gathering.finish()
        reducing.sent()


def middle_kernel(refs):
    place = Place()
    place.greet()
    middle(refs, place, Gather(place, refs.held, gather_stages(MIDDLE.values()), refs.gather))


def leave_weight(refs, j, made):
    def weight(index):
        grad = dot_tokens(refs.normed[...], refs.grad_packed[j, :, half(index)]).astype(BF16)
        put_columns(made, index, grad)

    loop(2, weight)


def leave_back(refs, j):
    def back(index):
        refs.grad_normed[:, half(index)] += dot_rows(
            refs.grad_packed[j], half_rows(refs.unit, index)
        )

    loop(2, back)


def leave_norm(refs, pump=lambda window: None):
    def join(window, at, mods, live):
        normal, root = centered(refs.tokens[at, :].astype(F32))
        grad_normed = refs.grad_normed[at, :]
        refs.grad_tokens[at, :] = refs.grad_middle[at, :] + norm_back(
            grad_normed, normal, root, mods[1]
        )
        add_sums(refs.sums, window, 0, grad_normed)
        add_sums(refs.sums, window, 1, grad_normed * normal)

    each_rows(refs.mod, refs.live, join, pump=pump)


def back_plain_kernel(refs):
    step = pl.program_id(0)

    @pl.when(step < H // 2)
    def _():
        attend_back_pair(refs, backward_pair(jnp.minimum(step, H // 2 - 1)))

    @pl.when(step == H // 2)
    def _():
        refs.sums[...] = jnp.zeros_like(refs.sums)
        refs.grad_normed[...] = jnp.zeros_like(refs.grad_normed)
        for j in range(3):
            fetch = pltpu.make_async_copy(refs.held.at[QKV + j], refs.unit, refs.fetch)
            fetch.start()
            leave_weight(refs, j, refs.made)
            put = pltpu.make_async_copy(refs.made, refs.part.at[j], refs.made_sem)
            put.start()
            fetch.wait()
            leave_back(refs, j)
            put.wait()
        leave_norm(refs)


def fold_spreads(refs):
    heads = H * WIDE // WSIDE
    shape_of = (WSIDE * LANES, TILE)
    place = lax.broadcasted_iota(jnp.int32, shape_of, 0)
    offset = lax.broadcasted_iota(jnp.int32, shape_of, 1)
    own, row, other = place // LANES, place // WSIDE % (LANES // WSIDE), place % WSIDE
    side_span = 2 * WSIDE - 1
    row_diff, col_diff = side_span - 1 - row, own - other + (WSIDE - 1)
    same = (row < side_span) & (row_diff * side_span + col_diff == offset)
    onto = jnp.where(same, 1.0, 0.0).astype(BF16)
    left = jnp.concatenate(
        [refs.spreads[pl.ds(own, heads, stride=WSIDE), :] for own in range(WSIDE)], axis=1
    )
    total = jnp.zeros((heads, TILE), F32)
    for _ in range(3):
        low = left.astype(BF16)
        total = total + dot(low, onto)
        left = left - low.astype(F32)
    rows = 2 * WIDE // WSIDE
    for block in range(8):
        refs.table[block // 2, block % 2] = total[block * rows : (block + 1) * rows]


def back_kernel(refs):
    place = Place()
    z, x, y, c = place.z, place.x, place.y, place.c
    step = pl.program_id(0)

    def buffers(unit):
        every = (EARLY + LATE).index(unit)
        late = every - len(EARLY)
        assert unit not in DONE
        if late < 0:
            core, side = None, refs.side_in.at[every - len(DONE)]
        else:
            core, side = refs.core.at[late], refs.side.at[late]
        if unit in REDUCE_ASIDE:
            return core, side, None, refs.aside.at[0]
        return core, side, refs.corner.at[every], refs.distant.at[every]

    def store(unit, part, values):
        if unit >= DOWN:
            first = part * 512 + (unit - DOWN) * LANES
            refs.grad_down[pl.ds(pl.multiple_of(first, LANES), LANES), :] = values
            return
        at = pl.ds(pl.multiple_of(part * HALF, HALF), HALF)
        if unit < OUT:
            column = picked(z * 2 + x, unit) * LANES
            refs.grad_qkv[at, pl.ds(pl.multiple_of(column, LANES), LANES)] = values
            return
        target, start = (refs.grad_out, OUT) if unit < UP else (refs.grad_up, UP)
        column = (unit - start) * LANES
        target[at, column : column + LANES] = values

    work = Reduce(
        place,
        lambda unit: refs.made.at[unit] if unit < OUT else refs.part.at[unit],
        LATE_POINTS,
        store,
        buffers,
        refs.reduce,
    )
    small = Copies(*refs.small)

    events = [(at, move) for at in sorted(LATE_POINTS) for move in LATE_POINTS[at]]

    def run(until):
        while events and events[0][0] < until:
            work.step(*events.pop(0)[1])

    for number in range(H // 2):

        @pl.when(step == number)
        def _(number=number):
            if number == 0:
                place.greet(EVERYONE)
            if number in (3, 6):
                leave_weight(refs, number // 3 - 1, refs.made.at[number // 3 - 1])
            run(number + 1)

    @pl.when(step < H // 2)
    def _():
        pair = backward_pair(jnp.minimum(step, H // 2 - 1))
        attend_back_pair(refs, pair)
        for head in range(2):
            at = pl.ds(pl.multiple_of((pair * 2 + head) * WIDE, WIDE), WIDE)
            refs.spreads[at, :] = refs.spread[head]

    @pl.when(step == H // 2)
    def _():
        for index, unit in enumerate(DONE):
            for part in range(2):
                store(unit, part, refs.done[index, part * HALF : (part + 1) * HALF, :])
        fold_spreads(refs)
        table = []
        for dz, dx, dy, dc in ALONG_ZX:
            source = refs.table.at[place.far(dz), 1 - x if dx else x]
            table.append(small(source, refs.table_zx.at[z, x], place.shifted(dz, dx, dy, dc)))
        refs.table_zx[z, x] = refs.table[z, x]
        refs.sums[...] = refs.late_sums[...]
        refs.grad_normed[...] = jnp.zeros_like(refs.grad_normed)

        def fetch(j):
            return pltpu.make_async_copy(refs.held.at[QKV + j], refs.unit, refs.fetch)

        fetch(0).start()
        leave_weight(refs, 2, refs.made.at[2])
        run(12)
        fetch(0).wait()
        leave_back(refs, 0)
        fetch(1).start()
        run(13)
        fetch(1).wait()
        leave_back(refs, 1)
        fetch(2).start()
        run(14)
        fetch(2).wait()
        leave_back(refs, 2)
        run(15)
        leave_norm(refs, lambda window: run(17 + window))
        for copy in table:
            copy.wait()
        total = refs.table_zx[0, 0]
        for block in range(1, 8):
            total = total + refs.table_zx[block // 2, block % 2]
        refs.table_own[...] = total
        refs.table_yc[y, c] = total
        table = [
            small(refs.table_own, refs.table_yc.at[y, c], place.shifted(*change))
            for change in ALONG_YC
        ]
        for block in range(48):
            which, column = divmod(block, 8)
            part = jnp.zeros((CLIP_ROWS, LANES), F32)
            for window in range(refs.mod.shape[0]):
                sums = refs.sums[window, which : which + 1, column * LANES : (column + 1) * LANES]
                part = part + refs.member[window] * sums
            first = block % 6 * CLIP_ROWS
            refs.clip[block // 12, block // 6 % 2, first : first + CLIP_ROWS, :] = part
        copies = []
        for dz, dx, dy, dc in ALONG_ZX:
            source = refs.clip.at[place.far(dz), 1 - x if dx else x]
            copies.append(small(source, refs.clip_zx.at[z, x], place.shifted(dz, dx, dy, dc)))
        refs.clip_zx[z, x] = refs.clip[z, x]
        run(19)
        for copy in copies:
            copy.wait()
        total = refs.clip_zx[0, 0]
        for block in range(1, 8):
            total = total + refs.clip_zx[block // 2, block % 2]
        refs.clip_own[...] = total
        refs.clip_yc[y, c] = total
        copies = [
            small(refs.clip_own, refs.clip_yc.at[y, c], place.shifted(*change))
            for change in ALONG_YC
        ]
        run(21)
        for copy in copies:
            copy.wait()
        total = refs.clip_yc[0, 0] + refs.clip_yc[0, 1] + refs.clip_yc[1, 0] + refs.clip_yc[1, 1]
        total = jnp.concatenate([total, jnp.zeros((8, LANES), F32)], axis=0)
        cond = jnp.zeros((8, SHARE), F32)
        lows = []
        for block in range(6):
            lows.append(total[block * CLIP_ROWS : block * CLIP_ROWS + 8].astype(BF16))
            lanes = slice(block * LANES, (block + 1) * LANES)
            cond = cond + dot_rows(lows[-1], refs.ada[:, lanes])
        clips = refs.condition.shape[0]
        refs.cond_own[...] = jnp.zeros_like(refs.cond_own)
        for row in range(2 * clips):
            clip, side = divmod(row, 2)
            refs.cond_own[row : row + 1, :] = cond[
                clip : clip + 1, side * LANES : (side + 1) * LANES
            ]
        refs.cond_all[z, x, y, c] = refs.cond_own[...]
        copies = [
            small(refs.cond_own, refs.cond_all.at[z, x, y, c], place.shifted(*change))
            for change in EVERYONE
        ]
        for block, low in enumerate(lows):
            lanes = slice(block * LANES, (block + 1) * LANES)
            refs.grad_ada[:, lanes] = dot_tokens(act_rows(refs, place), low)
            refs.grad_bias[block : block + 1, :] = jnp.sum(
                low[:CLIP_ROWS].astype(F32), axis=0, keepdims=True
            )
        run(23)
        for copy in table:
            copy.wait()
        total = refs.table_yc[0, 0] + refs.table_yc[0, 1] + refs.table_yc[1, 0] + refs.table_yc[1, 1]
        for head in range(2):
            for frame in range(FRAMES):
                first = (FRAMES - 1 - frame) * OFFSETS
                row = head * (WIDE // WSIDE) + frame
                refs.table_total[head : head + 1, first : first + OFFSETS] = total[
                    row : row + 1, :OFFSETS
                ]
        run(100)
        for copy in copies:
            copy.wait()
        for block in range(4):
            total = refs.cond_all[0, 0, block // 2, block % 2]
            for other in range(1, 8):
                total = total + refs.cond_all[other // 2, other % 2, block // 2, block % 2]
            for row in range(2 * clips):
                clip, side = divmod(row, 2)
                first = block * SHARE + side * LANES
                value = refs.condition[clip : clip + 1, first : first + LANES]
                gate = 1.0 / (1.0 + jnp.exp(-value))
                refs.grad_condition[clip : clip + 1, first : first + LANES] = (
                    total[row : row + 1] * gate * (1.0 + value * (1.0 - gate))
                )
        work.sent()


def enter_plain(tokens, held, mod):
    rows = tokens.shape[0]
    inputs = {"tokens": (tokens, vmem()), "held": (held, anywhere()), "mod": (mod, vmem())}
    outputs = {
        "normed": (shape(BF16, rows, D), vmem()),
        "packed": (shape(BF16, 3, rows, D), vmem()),
    }
    scratch = {
        "units": pltpu.VMEM((1, *SPLIT), BF16),
        "fetches": pltpu.SemaphoreType.DMA((1,)),
    }
    return call(enter_plain_kernel, "enter_plain", inputs, outputs, scratch)


def whole(array):
    return pl.BlockSpec(
        array.shape, lambda p: (0,) * len(array.shape), pipeline_mode=pl.Buffered(1)
    )


def result(dtype, *sizes):
    made = shape(dtype, *sizes)
    return made, whole(made)


def attend_probs(windows, first):
    def pair(step):
        return forward_pair(jnp.clip(step - first, 0, H // 2 - 1))

    return (
        shape(BF16, windows, H, WIN, WIN),
        pl.BlockSpec((windows, 2, WIN, WIN), lambda p: (0, pair(p), 0, 0)),
    )


def attend_scratch():
    return {"strip": pltpu.VMEM((2, CELLS, STRIP), F32), "bias": pltpu.VMEM((2, WIN, WIN), F32)}


def middle_outputs(rows):
    return {
        "output": (shape(BF16, rows, D), anywhere()),
        "grad_middle": (shape(F32, rows, D), anywhere()),
        "grad_mixed": (shape(BF16, rows, D), anywhere()),
        "sums": result(F32, rows // WIN, 8, D),
        "part": (shape(BF16, UNITS, *SPLIT), anywhere()),
    }


def middle_scratch(rows):
    return {
        "units": pltpu.VMEM((4, *SPLIT), BF16),
        "attended": pltpu.VMEM((rows, D), F32),
        "normed": pltpu.VMEM((rows, D), BF16),
        "result_sem": pltpu.SemaphoreType.DMA((3,)),
        "mlp": pltpu.VMEM((rows, D), F32),
        "grad_normed": pltpu.VMEM((rows, D), F32),
        "packed": pltpu.VMEM((3, rows, D), BF16),
        "made": pltpu.VMEM((2, *SPLIT), BF16),
        "fetches": pltpu.SemaphoreType.DMA((4,)),
        "made_sem": pltpu.SemaphoreType.DMA((2,)),
    }


def centre(special, live_frames, tokens, cotangent, mixed, mod, held):
    rows = tokens.shape[0]
    inputs = {
        name: (array, whole(array))
        for name, array in (
            ("tokens", tokens),
            ("cotangent", cotangent),
            ("mixed", mixed),
            ("mod", mod),
        )
    }
    inputs["live"] = (live_frames, smem())
    outputs, scratch = middle_outputs(rows), middle_scratch(rows)
    if not special:
        inputs["held"] = (held, anywhere())
        return call(middle, "middle_plain", inputs, outputs, scratch, grid=(1,), limit=60)
    inputs["held_in"] = (held, anywhere())
    outputs |= {
        "held": (shape(BF16, UNITS, *SPLIT), anywhere()),
        "side_out": result(BF16, *Reduce.side_shape(len(EARLY) - len(DONE))),
        "total": result(F32, len(DONE), SHARE, LANES),
    }
    scratch |= {
        "core": pltpu.VMEM(Reduce.core_shape(len(EARLY)), BF16),
        "side": pltpu.VMEM(Reduce.side_shape(len(EARLY)), BF16),
        "corner": pltpu.VMEM(Reduce.corner_shape(len(DONE)), BF16),
        "distant": pltpu.VMEM(Reduce.distant_shape(len(DONE)), BF16),
        "aside": pltpu.VMEM(Reduce.aside_shape(1), BF16),
        "reduce": Reduce.scratch(EARLY_POINTS),
        "gather": Gather.semaphores(gather_stages(MIDDLE.values())),
    }
    return call(
        middle_kernel,
        "middle",
        inputs,
        outputs,
        scratch,
        (("held_in", "held"),),
        collective=2,
        grid=(1,),
        limit=60,
    )


def begin(tokens, own, smalls):
    rows = tokens.shape[0]
    windows = rows // WIN
    inputs = {"tokens": (tokens, whole(tokens))}
    for name, block in zip(("qkv", "out", "up", "down"), own, strict=True):
        inputs[name] = (block, whole(block))
    for name, array in zip(("condition", "ada", "bias_in", "rel_table"), smalls[1:], strict=True):
        inputs[name] = (array, whole(array))
    inputs["frames"] = (smalls[0], smem())
    outputs = {
        "probs": attend_probs(windows, 1),
        "mixed_out": (shape(BF16, rows, D), anywhere()),
        "normed_out": (shape(BF16, rows, D), anywhere()),
        "packed_out": (shape(BF16, 3, rows, D), anywhere()),
        "held": (shape(BF16, UNITS, *SPLIT), anywhere()),
        "mod": result(F32, windows, 8, D),
        "member": result(F32, windows, CLIP_ROWS, LANES),
        "live": (shape(jnp.int32, windows), smem()),
    }
    stages = gather_stages(ENTER + tuple(ATTEND.values()))
    scratch = attend_scratch() | {
        "units": pltpu.VMEM((1, *SPLIT), BF16),
        "fetches": pltpu.SemaphoreType.DMA((1,)),
        "normed": pltpu.VMEM((rows, D), BF16),
        "packed": pltpu.VMEM((3, rows, D), BF16),
        "mixed": pltpu.VMEM((rows, D), BF16),
        "packed_sem": pltpu.SemaphoreType.DMA((5,)),
        "own": pltpu.VMEM((UNITS, SHARE, LANES), BF16),
        "own_sem": pltpu.SemaphoreType.DMA((UNITS,)),
        "gather": Gather.semaphores(stages),
        "small": [pltpu.SemaphoreType.DMA((18,))] * 2,
        "mod_part": pltpu.VMEM((MOD_ROWS, LANES), F32),
        "mod_parts": pltpu.VMEM((2, 2, MOD_ROWS, LANES), F32),
        "mods": pltpu.VMEM((4, 2, MOD_ROWS, LANES), F32),
        "rows": pltpu.VMEM((24, TILE), F32),
        "spread": pltpu.VMEM((2 * SPREAD, LANES), F32),
        "table_own": pltpu.VMEM((2, SPREAD, LANES), BF16),
        "table": pltpu.VMEM((4, 2, 2, SPREAD, LANES), BF16),
    }
    return call(
        start_kernel,
        "start",
        inputs,
        outputs,
        scratch,
        collective=0,
        grid=(H // 2 + 1,),
        limit=60,
    )


def deliver_kernel(refs):
    names = [name for name in vars(refs) if name.startswith("from_")]
    loads, stores = [], []
    for index, name in enumerate(names):
        plain = name[len("from_") :]
        held = getattr(refs, "held_" + plain)
        loads.append(pltpu.make_async_copy(getattr(refs, name), held, refs.sems.at[0, index]))
        stores.append(pltpu.make_async_copy(held, getattr(refs, plain), refs.sems.at[1, index]))
        loads[-1].start()
    for load, store in zip(loads, stores, strict=True):
        load.wait()
        store.start()
    for store in stores:
        store.wait()


def deliver(**arrays):
    inputs = {"from_" + name: (array, anywhere()) for name, array in arrays.items()}
    outputs = {name: (shape(array.dtype, *array.shape), anywhere()) for name, array in arrays.items()}
    scratch = {"held_" + name: pltpu.VMEM(array.shape, array.dtype) for name, array in arrays.items()}
    scratch["sems"] = pltpu.SemaphoreType.DMA((2, len(arrays)))
    return call(deliver_kernel, "deliver", inputs, outputs, scratch)


def attend_plain(packed, table, live_frames):
    windows = live_frames.shape[0]
    rows = windows * WIN
    inputs = {
        "live": (live_frames, smem()),
        "query": (packed, packed_block(0, rows, forward_pair)),
        "key": (packed, packed_block(1, rows, forward_pair)),
        "value": (packed, packed_block(2, rows, forward_pair)),
        "table": (table, pl.BlockSpec((2, SPREAD, LANES), lambda p: (forward_pair(p), 0, 0))),
    }
    return call(
        attend_plain_kernel,
        "attend_plain",
        inputs,
        {
            "mixed": (
                shape(BF16, rows, D),
                pl.BlockSpec((rows, LANES), lambda p: (0, forward_pair(p))),
            ),
            "probs": attend_probs(windows, 0),
        },
        attend_scratch(),
        grid=(H // 2,),
    )


def back(
    special, live_frames, tokens, mod, packed, normed, probs, mid, held, ada, member, condition
):
    window_count = probs.shape[0]
    rows = window_count * WIN
    pairs = H // 2

    def last(step):
        return backward_pair(jnp.minimum(step, pairs - 1))

    def packed_pair(which):
        return packed_block(which, rows, last)

    inputs = {
        "live": (live_frames, smem()),
        "query": (packed, packed_pair(0)),
        "key": (packed, packed_pair(1)),
        "value": (packed, packed_pair(2)),
        "probs": (
            probs,
            pl.BlockSpec((window_count, 2, WIN, WIN), lambda p: (0, last(p), 0, 0)),
        ),
        "grad": (mid.grad_mixed, pl.BlockSpec((rows, LANES), lambda p: (0, last(p)))),
        "held": (held, anywhere()),
    }
    for name, array in (
        ("tokens", tokens),
        ("mod", mod),
        ("normed", normed),
        ("grad_middle", mid.grad_middle),
    ):
        inputs[name] = (array, whole(array))

    outputs = {"grad_tokens": result(F32, rows, D)}
    scratch = {
        "strip": pltpu.VMEM((2, CELLS, STRIP), F32),
        "grad_packed": pltpu.VMEM((3, rows, D), BF16),
        "unit": pltpu.VMEM(SPLIT, BF16),
        "grad_normed": pltpu.VMEM((rows, D), F32),
        "fetch": pltpu.SemaphoreType.DMA,
    }
    if not special:
        outputs["sums"] = result(F32, window_count, 8, D)
        outputs["part"] = (shape(BF16, 3, *SPLIT), anywhere())
        outputs["spread"] = (
            shape(F32, H, SPREAD, LANES),
            pl.BlockSpec((2, SPREAD, LANES), lambda p: (last(p), 0, 0)),
        )
        scratch["made"] = pltpu.VMEM(SPLIT, BF16)
        scratch["made_sem"] = pltpu.SemaphoreType.DMA
        return call(
            back_plain_kernel, "back_plain", inputs, outputs, scratch, grid=(pairs + 1,)
        )
    inputs |= {
        "late_sums": (mid.sums, whole(mid.sums)),
        "ada": (ada, whole(ada)),
        "condition": (condition, whole(condition)),
        "member": (member, whole(member)),
        "side_in": (mid.side_out, whole(mid.side_out)),
        "done": (mid.total, whole(mid.total)),
        "part": (mid.part, anywhere()),
    }
    outputs |= {
        "grad_qkv": result(F32, SHARE, 3 * LANES),
        "grad_out": result(F32, SHARE, LANES),
        "grad_up": result(F32, SHARE, 4 * LANES),
        "grad_down": result(F32, 4 * SHARE, LANES),
        "grad_ada": result(F32, SHARE, 6 * LANES),
        "grad_bias": result(F32, 6, LANES),
        "grad_condition": result(F32, *condition.shape),
        "table_total": result(F32, 2, REL),
    }
    count, late = len(EARLY + LATE), len(LATE)
    scratch |= {
        "spread": pltpu.VMEM((2, WIDE, LANES), F32),
        "spreads": pltpu.VMEM((H * WIDE, LANES), F32),
        "made": pltpu.VMEM((3, *SPLIT), BF16),
        "sums": pltpu.VMEM((window_count, 8, D), F32),
        "core": pltpu.VMEM(Reduce.core_shape(late), BF16),
        "side": pltpu.VMEM(Reduce.side_shape(late), BF16),
        "corner": pltpu.VMEM(Reduce.corner_shape(count), BF16),
        "distant": pltpu.VMEM(Reduce.distant_shape(count), BF16),
        "aside": pltpu.VMEM(Reduce.aside_shape(1), BF16),
        "reduce": Reduce.scratch(LATE_POINTS),
        "table": pltpu.VMEM((4, 2, 2 * WIDE // WSIDE, TILE), F32),
        "table_zx": pltpu.VMEM((4, 2, 2 * WIDE // WSIDE, TILE), F32),
        "table_own": pltpu.VMEM((2 * WIDE // WSIDE, TILE), F32),
        "table_yc": pltpu.VMEM((2, 2, 2 * WIDE // WSIDE, TILE), F32),
        "clip": pltpu.VMEM((4, 2, MOD_ROWS, LANES), F32),
        "clip_zx": pltpu.VMEM((4, 2, MOD_ROWS, LANES), F32),
        "clip_own": pltpu.VMEM((MOD_ROWS, LANES), F32),
        "clip_yc": pltpu.VMEM((2, 2, MOD_ROWS, LANES), F32),
        "cond_own": pltpu.VMEM((8, LANES), F32),
        "cond_all": pltpu.VMEM((4, 2, 2, 2, 8, LANES), F32),
        "small": [pltpu.SemaphoreType.DMA((51,))] * 2,
    }
    return call(
        back_kernel,
        "back",
        inputs,
        outputs,
        scratch,
        collective=3,
        grid=(pairs + 1,),
        limit=60,
    )


def per_device(
    special,
    tokens,
    condition,
    clip_frames,
    ada_weight,
    ada_bias,
    qkv_weight,
    out_weight,
    up_weight,
    down_weight,
    rel_table,
    cotangent,
):
    window_count = tokens.shape[0]
    clip_count = condition.shape[0]
    rows_ada, cols_ada = ada_weight.shape
    token_rows = tokens.reshape(window_count * WIN, D)
    cotangent_rows = cotangent.reshape(window_count * WIN, D)
    own = (qkv_weight, out_weight, up_weight, down_weight)
    if special:
        smalls = (clip_frames, condition, ada_weight, ada_bias.reshape(1, cols_ada), rel_table)
        start = across = begin(token_rows, own, smalls)
        mixed = start.mixed_out
        live_frames, member_wide, mod = start.live, start.member, start.mod
        packed, held, normed = start.packed_out, start.held, start.normed_out
    else:
        row_block = lax.axis_index("fsdp")
        col_block = lax.axis_index("dp")
        first_window = lax.axis_index(("dp", "fsdp")) * window_count
        live_frames, member_int = window_layout(clip_frames, first_window, window_count)
        member = member_int.astype(F32)
        activity_low = jax.nn.silu(condition).astype(BF16)
        rows_own = lax.dynamic_slice_in_dim(activity_low, row_block * rows_ada, rows_ada, 1)
        mod_part = jnp.dot(rows_own, ada_weight, preferred_element_type=F32)
        clip_mod = lax.all_gather(lax.psum(mod_part, "fsdp"), "dp", axis=1, tiled=True)
        bias = lax.all_gather(ada_bias, "dp", axis=0, tiled=True)
        clip_mod = clip_mod + bias.astype(F32)[None, :]
        member_wide = None
        window_mod = jnp.sum(member[:, :, None] * clip_mod[None], axis=1)
        window_mod = jnp.pad(window_mod.reshape(window_count, 6, D), ((0, 0), (0, 2), (0, 0)))
        whole = [
            lax.all_gather(
                lax.all_gather(weight, "dp", axis=1, tiled=True), "fsdp", axis=0, tiled=True
            )
            for weight in own
        ]
        held = units_of(*whole).reshape(UNITS, *SPLIT)
        mod = window_mod
        start = enter_plain(token_rows, held, mod)
        packed, normed = start.packed, start.normed
        table = spread_table(lax.all_gather(rel_table, "dp", axis=0, tiled=True))
        across = attend_plain(packed, table, live_frames)
        mixed = across.mixed
    mid = centre(special, live_frames, token_rows, cotangent_rows, mixed, mod, held)
    held = mid.held if special else held
    end = back(
        special,
        live_frames,
        token_rows,
        mod,
        packed,
        normed,
        across.probs,
        mid,
        held,
        ada_weight,
        member_wide,
        condition,
    )
    if special:
        end = deliver(
            output=mid.output,
            grad_tokens=end.grad_tokens,
            grad_condition=end.grad_condition,
            grad_ada=end.grad_ada,
            grad_bias=end.grad_bias,
            grad_qkv=end.grad_qkv,
            grad_out=end.grad_out,
            grad_up=end.grad_up,
            grad_down=end.grad_down,
            table=end.table_total,
        )
        return (
            end.output.reshape(tokens.shape),
            end.grad_tokens.reshape(tokens.shape),
            end.grad_condition,
            end.grad_ada,
            end.grad_bias.reshape(cols_ada),
            end.grad_qkv,
            end.grad_out,
            end.grad_up,
            end.grad_down,
            end.table,
        )
    part = jnp.concatenate([end.part, mid.part[OUT:]])
    grads = [
        lax.psum_scatter(
            lax.psum_scatter(grad, "fsdp", scatter_dimension=0, tiled=True),
            "dp",
            scatter_dimension=1,
            tiled=True,
        ).astype(F32)
        for grad in weights_of(part.reshape(UNITS, 8, D, LANES))
    ]
    grad_mod = (mid.sums + end.sums)[:, :6].reshape(window_count, 6 * D)
    clip_part = lax.dot_general(
        member,
        grad_mod,
        (((0,), (0,)), ((), ())),
        precision=HIGHEST,
        preferred_element_type=F32,
    )
    clip_sum, table_sum = lax.psum((clip_part, gather_table(end.spread)), ("dp", "fsdp"))
    clip_cols = lax.dynamic_slice_in_dim(
        clip_sum.astype(BF16), col_block * cols_ada, cols_ada, 1
    )
    heads_own = rel_table.shape[0]
    table_grad = lax.dynamic_slice_in_dim(table_sum, col_block * heads_own, heads_own, 0)
    cond_part = lax.dot_general(
        clip_cols, ada_weight, (((1,), (1,)), ((), ())), preferred_element_type=F32
    )
    cond_total = lax.all_gather(lax.psum(cond_part, "dp"), "fsdp", axis=1, tiled=True)
    grad_ada_weight = lax.dot_general(
        rows_own, clip_cols, (((0,), (0,)), ((), ())), preferred_element_type=F32
    )
    grad_ada_bias = jnp.sum(clip_cols.astype(F32), axis=0)
    _, silu_back = jax.vjp(jax.nn.silu, condition)
    return (
        mid.output.reshape(tokens.shape),
        end.grad_tokens.reshape(tokens.shape),
        silu_back(cond_total)[0],
        grad_ada_weight,
        grad_ada_bias,
        *grads,
        table_grad,
    )


def solution(mesh):
    special = dict(mesh.shape) == {"dp": 8, "fsdp": 4}
    both = P(("dp", "fsdp"), None, None)
    weight = P("fsdp", "dp")
    in_specs = (both, P(), P(), weight, P("dp")) + (weight,) * 4 + (P("dp", None), both)
    out_specs = (both, both, P(), weight, P("dp")) + (weight,) * 4 + (P("dp", None),)
    return jax.shard_map(
        functools.partial(per_device, special),
        mesh=mesh,
        in_specs=in_specs,
        out_specs=out_specs,
        check_vma=False,
    )
```

profile of v0, /device:TPU:0, one launch (start us, length us, event | category | flops | bytes accessed | tf_op | source)
XLA Modules:
  0.0 279.6 jit_solution(6683783161764535106)
XLA Ops:
  0.6 1.3 reshape.40.refs_7_
  1.9 89.2 %start.1 = (bf16[2,16,320,320]{3,2,1,0:T(8,128)(2,1)}, bf16[640,1024]{1,0:T(8,128)(2,1)}, bf16[640,1024]{1,0:T(8,128)(2,1)}, bf16[3,640,1024]{2,1,0:T(8,128)(2,1...) custom-call(bf16[640,1024]{1,0:T(8,128)(2,1)} %bitcast.5, ...), custom_call_target="tpu_custom_call" | custom-call | tf_op jit(solution)/shard_map/start/pallas_call | solution.py:615
  91.1 93.8 %middle.1 = (bf16[640,1024]{1,0:T(8,128)(2,1)}, f32[640,1024]{1,0:T(8,128)}, bf16[640,1024]{1,0:T(8,128)(2,1)}, f32[2,8,1024]{2,1,0:T(8,128)}, bf16[12,4,2,2,2,2...) custom-call(bf16[640,1024]{1,0:T(8,128)(2,1)} %bitcast.6, ...), custom_call_target="tpu_custom_call", output_to_operand_aliasing={{5}: (5, {})} | custom-call | tf_op jit(solution)/shard_map/middle/pallas_call | solution.py:617
  184.9 89.7 %back.1 = (f32[640,1024]{1,0:T(8,128)}, f32[256,384]{1,0:T(8,128)}, f32[256,128]{1,0:T(8,128)}, f32[256,512]{1,0:T(8,128)}, f32[1024,128]{1,0:T(8,128)}, /*index...) custom-call(s32[2]{0:T(128)} %get-tuple-element.47.refs_4_.refs_0_, ...), custom_call_target="tpu_custom_call" | custom-call | tf_op jit(solution)/shard_map/back/pallas_call | solution.py:617
  274.6 4.8 %deliver.1 = (bf16[640,1024]{1,0:T(8,128)(2,1)}, f32[640,1024]{1,0:T(8,128)}, f32[3,1024]{1,0:T(4,128)}, f32[256,768]{1,0:T(8,128)}, f32[6,128]{1,0:T(8,128)}, /...) custom-call(bf16[640,1024]{1,0:T(8,128)(2,1)} %get-tuple-element.49., ...), custom_call_target="tpu_custom_call" | custom-call | tf_op jit(solution)/shard_map/deliver/pallas_call | solution.py:617
where the time goes:
time: 284 us; the launch traced here: 280 us
  Pallas kernels  278 us (98%)
    pallas_call x4, Pallas kernels, call(): result = made()(*arrays)  278 us

commit v1 on v0

--- a/solution.py
+++ b/solution.py
@@ -1462,7 +1462,7 @@
         "output": (shape(BF16, rows, D), anywhere()),
         "grad_middle": (shape(F32, rows, D), anywhere()),
         "grad_mixed": (shape(BF16, rows, D), anywhere()),
-        "sums": result(F32, rows // WIN, 8, D),
+        "sums": (shape(F32, rows // WIN, 8, D), vmem()),
         "part": (shape(BF16, UNITS, *SPLIT), anywhere()),
     }
 
@@ -1485,7 +1485,7 @@
 def centre(special, live_frames, tokens, cotangent, mixed, mod, held):
     rows = tokens.shape[0]
     inputs = {
-        name: (array, whole(array))
+        name: (array, vmem())
         for name, array in (
             ("tokens", tokens),
             ("cotangent", cotangent),
@@ -1497,12 +1497,12 @@
     outputs, scratch = middle_outputs(rows), middle_scratch(rows)
     if not special:
         inputs["held"] = (held, anywhere())
-        return call(middle, "middle_plain", inputs, outputs, scratch, grid=(1,), limit=60)
+        return call(middle, "middle_plain", inputs, outputs, scratch, limit=60)
     inputs["held_in"] = (held, anywhere())
     outputs |= {
         "held": (shape(BF16, UNITS, *SPLIT), anywhere()),
-        "side_out": result(BF16, *Reduce.side_shape(len(EARLY) - len(DONE))),
-        "total": result(F32, len(DONE), SHARE, LANES),
+        "side_out": (shape(BF16, *Reduce.side_shape(len(EARLY) - len(DONE))), vmem()),
+        "total": (shape(F32, len(DONE), SHARE, LANES), vmem()),
     }
     scratch |= {
         "core": pltpu.VMEM(Reduce.core_shape(len(EARLY)), BF16),
@@ -1521,7 +1521,6 @@
         scratch,
         (("held_in", "held"),),
         collective=2,
-        grid=(1,),
         limit=60,
     )
 

time: 284 us -> 284 us (level)
  no operation moved by 1% of the time
where the time goes in v1:
time: 284 us; the launch traced here: 280 us
  Pallas kernels  278 us (98%)
    pallas_call x4, Pallas kernels, call(): result = made()(*arrays)  278 us

profile of v1, /device:TPU:0, one launch (start us, length us, event | category | flops | bytes accessed | tf_op | source)
XLA Modules:
  0.0 279.6 jit_solution(6683783161764535106)
XLA Ops:
  0.6 1.3 reshape.40.refs_7_
  1.9 89.2 %start.1 = (bf16[2,16,320,320]{3,2,1,0:T(8,128)(2,1)}, bf16[640,1024]{1,0:T(8,128)(2,1)}, bf16[640,1024]{1,0:T(8,128)(2,1)}, bf16[3,640,1024]{2,1,0:T(8,128)(2,1...) custom-call(bf16[640,1024]{1,0:T(8,128)(2,1)} %bitcast.5, ...), custom_call_target="tpu_custom_call" | custom-call | tf_op jit(solution)/shard_map/start/pallas_call | solution.py:615
  91.1 93.8 %middle.1 = (bf16[640,1024]{1,0:T(8,128)(2,1)}, f32[640,1024]{1,0:T(8,128)}, bf16[640,1024]{1,0:T(8,128)(2,1)}, f32[2,8,1024]{2,1,0:T(8,128)}, bf16[12,4,2,2,2,2...) custom-call(bf16[640,1024]{1,0:T(8,128)(2,1)} %bitcast.6, ...), custom_call_target="tpu_custom_call", output_to_operand_aliasing={{5}: (5, {})} | custom-call | tf_op jit(solution)/shard_map/middle/pallas_call | solution.py:617
  184.9 89.7 %back.1 = (f32[640,1024]{1,0:T(8,128)}, f32[256,384]{1,0:T(8,128)}, f32[256,128]{1,0:T(8,128)}, f32[256,512]{1,0:T(8,128)}, f32[1024,128]{1,0:T(8,128)}, /*index...) custom-call(s32[2]{0:T(128)} %get-tuple-element.47.refs_4_.refs_0_, ...), custom_call_target="tpu_custom_call" | custom-call | tf_op jit(solution)/shard_map/back/pallas_call | solution.py:617
  274.6 4.8 %deliver.1 = (bf16[640,1024]{1,0:T(8,128)(2,1)}, f32[640,1024]{1,0:T(8,128)}, f32[3,1024]{1,0:T(4,128)}, f32[256,768]{1,0:T(8,128)}, f32[6,128]{1,0:T(8,128)}, /...) custom-call(bf16[640,1024]{1,0:T(8,128)(2,1)} %get-tuple-element.49., ...), custom_call_target="tpu_custom_call" | custom-call | tf_op jit(solution)/shard_map/deliver/pallas_call | solution.py:617
